TPU v7x, 128 devices: a whole 4x4x4 slice. The times are simulated.
128 devices in a mesh: dp: 4 (over x), vocab: 32 (over z, y, core).
Axes of the slice: x: 4, y: 4, z: 4, core: 2. Of those that a mesh axis runs over, the one named last changes fastest.
Arguments:
- hidden: bfloat16 [1024, 2304], P('dp', 'vocab'), may hold values from -6 to 6
- embed: bfloat16 [128000, 2304], P('vocab')
- token_ids: int32 [1024], P('dp'), may hold values from 0 to 127999
- lookup_cot: bfloat16 [1024, 2304], P('dp', 'vocab'), may hold values from -0.15625 to 0.15625
- teacher_ids: int32 [1024, 64], P(('dp', 'vocab')), may hold values from 0 to 127999, as said below
- teacher_logits: float32 [1024, 64], P(('dp', 'vocab')), may hold values from -8 to 8
Outputs:
- hidden_grad: bfloat16 [1024, 2304], P('dp', 'vocab')
- embed_grad: bfloat16 [128000, 2304], P('vocab', 'dp')
- divergence: float32 [1024], P(('dp', 'vocab'))
Inputs may be any that keep to these rules, and one draw needn't show every extreme that they name: `teacher_ids`: each token's 64 teacher ids are different.
All inputs are finite; a program needn't handle non-finite values.
Results may differ from a plain program's by a relative error of at most 0.0043.
The roundings to bfloat16 on the way count: a program that leaves them out, or rounds other values in their place, can miss the bound.
Values may be sent and summed in bfloat16 or wider, within the bound.
No kernel may reach another device: no remote copies, remote signals or barrier semaphores. Data moves between devices by JAX's collectives and lax.ppermute only.
A program may use at most 192 MiB of HBM per device.

v0:
```python
import math

import jax
import jax.numpy as jnp
from jax import lax
from jax.sharding import PartitionSpec as P

soft_cap = 30.0
loss_scale = 16.0


def divergence_of(teacher_prob, term, total):
    return jnp.sum(teacher_prob * jnp.log(teacher_prob), axis=1) - term + jnp.log(total)


def build_target(column, teacher_prob, row_count):
    group = column.shape[1] // 8
    row_iota = jnp.arange(row_count, dtype=jnp.int32)[None, None, :]
    target = jnp.zeros((column.shape[0], row_count), jnp.float32)
    for batch in range(8):
        cols = column[:, batch * group : (batch + 1) * group]
        probs = teacher_prob[:, batch * group : (batch + 1) * group]
        match = cols[:, :, None] == row_iota
        target = target + jnp.sum(jnp.where(match, probs[:, :, None], 0.0), axis=1)
    return target


def per_device(hidden, embed, token_ids, lookup_cot, teacher_ids, teacher_logits):
    row_count = embed.shape[0]
    width = embed.shape[1]
    vocab_size = lax.axis_size("vocab")
    offset = lax.axis_index("vocab") * row_count
    features, cot_full = (
        lax.all_gather(hidden, "vocab", axis=1, tiled=True),
        lax.all_gather(lookup_cot, "vocab", axis=1, tiled=True),
    )
    ids_full, logit_full = (
        lax.all_gather(teacher_ids, "vocab", axis=0, tiled=True),
        lax.all_gather(teacher_logits, "vocab", axis=0, tiled=True),
    )
    tokens_here = features.shape[0]
    share_len = tokens_here // vocab_size
    share_start = lax.axis_index("vocab") * share_len
    teacher_prob = jax.nn.softmax(logit_full, axis=1)
    raw = lax.dot_general(
        features, embed, (((1,), (1,)), ((), ())), preferred_element_type=jnp.float32
    )
    logits = soft_cap * jnp.tanh(raw / soft_cap)
    exp_terms = jnp.exp(logits)
    column = ids_full - offset
    target = build_target(column, teacher_prob, row_count)
    part_total = jnp.sum(exp_terms, axis=1)
    part_term = jnp.sum(target * logits, axis=1)
    total, term = lax.psum((part_total, part_term), "vocab")
    divergence = lax.dynamic_slice_in_dim(
        divergence_of(teacher_prob, term, total), share_start, share_len, 0
    )
    ratio = logits / soft_cap
    grads = (loss_scale * (exp_terms / total[:, None] - target) * (1.0 - ratio * ratio)).astype(
        jnp.bfloat16
    )
    summed = lax.psum_scatter(
        lax.dot_general(embed, grads, (((0,), (1,)), ((), ())), preferred_element_type=jnp.float32),
        "vocab",
        scatter_dimension=0,
        tiled=True,
    )
    hidden_grad = summed.T.astype(jnp.bfloat16)
    lookup_scale = math.sqrt(width)
    row_ids = offset + jnp.arange(row_count, dtype=jnp.int32)
    onehot = (token_ids[:, None] == row_ids[None, :]).astype(jnp.bfloat16)
    first_term = lax.dot_general(
        grads, features, (((0,), (0,)), ((), ())), preferred_element_type=jnp.float32
    )
    second_term = lax.dot_general(
        onehot, cot_full, (((0,), (0,)), ((), ())), preferred_element_type=jnp.float32
    )
    partial_rows = first_term + lookup_scale * second_term
    embed_grad = lax.psum_scatter(partial_rows, "dp", scatter_dimension=1, tiled=True).astype(
        jnp.bfloat16
    )
    return (hidden_grad, embed_grad, divergence)


def solution(mesh):
    placed = (
        P("dp", "vocab"),
        P("vocab", None),
        P("dp"),
        P("dp", "vocab"),
        P(("dp", "vocab"), None),
        P(("dp", "vocab"), None),
    )
    return jax.shard_map(
        per_device,
        mesh=mesh,
        in_specs=placed,
        out_specs=(P("dp", "vocab"), P("vocab", "dp"), P(("dp", "vocab"))),
        check_vma=False,
    )
```

profile of v0, /device:TPU:0, one launch (start us, length us, event | category | flops | bytes accessed | tf_op | source)
XLA Modules:
  0.0 621.6 jit_solution(3112334692809738993)
XLA Ops:
  7.2 0.7 all-gather.3.cloned.1.call-update
  7.9 0.7 all-gather.5.cloned.1.call-update
  8.7 26.2 %all_gather.14 = f32[256,64]{1,0:T(8,128)S(1)} all-gather(f32[8,64]{1,0:T(8,128)} %param.11), channel_id=1, replica_groups=mesh['dp'=4,'vocab'=32] {'vocab'}, dimensions={0}, use_global_device_ids=true | all-gather | bytes 67584 | tf_op jit(solution)/shard_map/all_gather | solution.py:39
  34.9 0.1 reduce_max.9
  35.0 0.2 fusion.6
  35.2 0.2 fusion.4
  35.4 24.0 %all_gather.13 = s32[256,64]{1,0:T(8,128)S(1)} all-gather(s32[8,64]{1,0:T(8,128)} %param.10), channel_id=1, replica_groups=mesh['dp'=4,'vocab'=32] {'vocab'}, dimensions={0}, use_global_device_ids=true | all-gather | bytes 67584 | tf_op jit(solution)/shard_map/all_gather | solution.py:38
  59.5 0.3 fusion.8
  60.1 0.1 copy.19
  60.1 0.1 copy.17
  60.3 0.3 fusion.9
  60.7 0.1 copy.26
  60.9 0.1 copy.20
  61.1 0.1 copy.16
  61.1 0.1 copy.12
  61.2 11.7 %select_reduce_fusion.6 = (f32[256,4000]{0,1:T(8,128)}, f32[256,4000]{0,1:T(8,128)}) fusion(f32[256,8]{0,1:T(8,128)S(1)} %copy.14, s32[256,8]{0,1:T(8,128)S(1)} %copy.13, f32[256,8]{0,1:T(8,128)S(1)} %copy.12, s32[256,8]{0,1:T(8,128)S(1)} %copy.11), kind=kLoop, calls=%fused_computation.13 | loop fusion | flops 47104000 | bytes 8224768 | tf_op jit(solution)/shard_map/reduce_sum | solution.py:24
  73.0 11.9 %select_reduce_fusion.4 = (f32[256,4000]{0,1:T(8,128)}, f32[256,4000]{0,1:T(8,128)}) fusion(f32[256,8]{0,1:T(8,128)S(1)} %copy.18, s32[256,8]{0,1:T(8,128)S(1)} %copy.17, f32[256,8]{0,1:T(8,128)S(1)} %copy.16, s32[256,8]{0,1:T(8,128)S(1)} %copy.15), kind=kLoop, calls=%fused_computation.9 | loop fusion | flops 47104000 | bytes 8224768 | tf_op jit(solution)/shard_map/reduce_sum | solution.py:24
  84.9 11.9 %select_reduce_fusion.2 = (f32[256,4000]{0,1:T(8,128)}, f32[256,4000]{0,1:T(8,128)}) fusion(f32[256,8]{0,1:T(8,128)S(1)} %copy.22, s32[256,8]{0,1:T(8,128)S(1)} %copy.21, f32[256,8]{0,1:T(8,128)S(1)} %copy.20, s32[256,8]{0,1:T(8,128)S(1)} %copy.19), kind=kLoop, calls=%fused_computation.5 | loop fusion | flops 47104000 | bytes 8224768 | tf_op jit(solution)/shard_map/reduce_sum | solution.py:24
  96.8 11.9 %select_reduce_fusion = (f32[256,4000]{0,1:T(8,128)}, f32[256,4000]{0,1:T(8,128)}) fusion(f32[256,8]{0,1:T(8,128)S(1)} %copy.26, s32[256,8]{0,1:T(8,128)S(1)} %copy.25, f32[256,8]{0,1:T(8,128)S(1)} %copy.24, s32[256,8]{0,1:T(8,128)S(1)} %copy.23), kind=kLoop, calls=%fused_computation.1 | loop fusion | flops 47104000 | bytes 8224768 | tf_op jit(solution)/shard_map/reduce_sum | solution.py:24
  108.7 21.8 %multiply_reduce_fusion = (f32[256]{0:T(256)S(1)}, f32[256]{0:T(256)S(1)}, f32[256,4000]{0,1:T(8,128)}, f32[256,4000]{0,1:T(8,128)}) fusion(f32[256,4000]{0,1:T(8,128)} %get-tuple-element.36, f32[256,4000]{0,1:T(8,128)} %get-tuple-element.37, f32[256,4000]{0,1:T(8,128)} %get-tuple-element.38, f32[256,4000]{0,1:T(8,128)} %get-tuple-element.39, ...), kind=kOutput, calls=%fused_computation.21 | convolution fusion | flops 4730880000 | bytes 60573696 | tf_op jit(solution)/shard_map/dot_general | solution.py:45
  130.5 65.4 %all-reduce = (f32[256]{0:T(256)S(1)}, f32[256]{0:T(256)S(1)}) all-reduce(f32[256]{0:T(256)S(1)} %get-tuple-element.13, f32[256]{0:T(256)S(1)} %get-tuple-element.12), channel_id=1, replica_groups=mesh['dp'=4,'vocab'=32] {'vocab'}, use_global_device_ids=true, to_apply=%region_1.0 | all-reduce | flops 512 | bytes 4096 | tf_op jit(solution)/shard_map/psum | solution.py:54
  195.9 4.7 multiply_convert_fusion
  200.5 10.3 %convolution_bitcast_fusion = f32[2304,256]{0,1:T(8,128)} fusion(bf16[256,4000]{0,1:T(8,128)(2,1)S(1)} %multiply_convert_fusion, bf16[4000,2304]{1,0:T(8,128)(2,1)} %param.7), kind=kOutput, calls=%fused_computation.20 | convolution fusion | flops 4718592000 | bytes 22839296 | tf_op jit(solution)/shard_map/dot_general | solution.py:63
  210.9 3.2 copy.28
  214.1 15.2 %fusion.10 = f32[4000,2304]{0,1:T(8,128)} fusion(bf16[256,4000]{0,1:T(8,128)(2,1)S(1)} %multiply_convert_fusion, bf16[256,2304]{0,1:T(8,128)(2,1)S(1)} %copy-done), kind=kOutput, calls=%fused_computation.38 | convolution fusion | flops 4718592000 | bytes 40091648 | tf_op jit(solution)/shard_map/dot_general | solution.py:72
  229.4 24.8 %multiply_add_fusion = f32[4000,2304]{0,1:T(8,128)} fusion(f32[4000,2304]{0,1:T(8,128)} %fusion.10, bf16[256,2304]{0,1:T(8,128)(2,1)} %all-gather.5.cloned.1.call-done, s32[4000]{0:T(1024)S(1)} %iota_add_fusion, s32[256]{0:T(256)S(1)} %copy-done.1), kind=kOutput, calls=%fused_computation | convolution fusion | flops 4738048000 | bytes 74924672 | tf_op jit(solution)/shard_map/dot_general | solution.py:75
  254.2 0.6 dynamic_slice.3
  254.8 35.1 %reduce-scatter.7.cloned.1.call-done = f32[72,256]{1,0:T(8,128)} async-done(((f32[2304,256]{1,0:T(8,128)}), f32[72,256]{1,0:T(8,128)}) %reduce-scatter.7.cloned.1.call-update) | async-done | bytes 73744
  289.9 1.0 copy.29
  290.9 0.7 copy.27
  291.6 316.5 %reduce-scatter.5.cloned.1.call-done = f32[4000,576]{0,1:T(8,128)} async-done(((f32[4000,2304]{0,1:T(8,128)}), f32[4000,576]{0,1:T(8,128)}) %reduce-scatter.5.cloned.1.call-update) | async-done | bytes 9216016 | tf_op jit(solution)/shard_map/reduce_scatter | solution.py:79
  608.1 6.6 %convert_element_type.16 = bf16[4000,576]{0,1:T(8,128)(2,1)} convert(f32[4000,576]{0,1:T(8,128)} %reduce-scatter.5.cloned.1.call-done) | non-fusion elementwise | flops 2304000 | bytes 13824000 | tf_op jit(solution)/shard_map/convert_element_type | solution.py:79
  (25 shorter events, 0.9 us)
Async XLA Ops:
  7.2 101.5 %all-gather.3.cloned.1.call-start = ((), (), s32[]{:S(2)}) async-start(), calls=%async_computation.2 | async-start | bytes 1216512 | tf_op jit(solution)/shard_map/all_gather | solution.py:34
  7.9 221.5 %all-gather.5.cloned.1.call-start = ((), (), s32[]{:S(2)}) async-start(), calls=%async_computation.3 | async-start | bytes 1216512 | tf_op jit(solution)/shard_map/all_gather | solution.py:35
  8.6 281.2 %reduce-scatter.7.cloned.1.call-start = ((), (), s32[]{:S(2)}) async-start(), calls=%async_computation.5 | async-start | bytes 2433024
  210.9 3.2 copy-start
  214.1 15.3 %copy-start.1 = (s32[256]{0:T(256)S(1)}, s32[256]{0:T(256)}, u32[]{:S(2)}) copy-start(s32[256]{0:T(256)} %param.8) | copy-start | bytes 3076
  214.1 394.1 %reduce-scatter.5.cloned.1.call-start = ((), (), s32[]{:S(2)}) async-start(), calls=%async_computation.4 | async-start | bytes 47185920 | tf_op jit(solution)/shard_map/reduce_scatter | solution.py:79
Sparse Core Ops, SparseCore 0:
  10.3 45.5 all-gather.2
  58.2 42.3 all-gather.4
  214.2 75.6 reduce-scatter.6
  292.4 315.7 reduce-scatter.4
where the time goes:
time: 632 us; the launch traced here: 622 us
  waiting for transfers between devices  353 us (56%)
  blocking collectives  116 us (18%)
  matrix products  72.2 us (11%)
  other arithmetic  59.3 us (9%)
  between operations  14.2 us (2%)
  local copies, waits for them, and re-layouts  7.19 us (1%)
    reduce_scatter x1, waiting for transfers between devices, per_device(): lax.psum_scatter(partial_rows, 'dp', scatter_dimension=1, tiled=True)  317 us
    psum x1, blocking collectives, per_device(): total, term = lax.psum((part_total, part_term), 'vocab')  65.4 us
    reduce_sum x4, other arithmetic, build_target(): target = target + jnp.sum(jnp.where(match, probs[:, :, None], 0.0), axis=1)  47.5 us
    unnamed x5, waiting for transfers between devices  36.5 us
    all_gather x1, blocking collectives, per_device(): lax.all_gather(teacher_logits, 'vocab', axis=0, tiled=True)  26.2 us
    dot_general x1, matrix products, per_device(): lax.dot_general(onehot, cot_full, (((0,), (0,)), ((), ())), preferred_ele...  24.8 us
    all_gather x1, blocking collectives, per_device(): lax.all_gather(teacher_ids, 'vocab', axis=0, tiled=True)  24 us
    dot_general x1, matrix products, per_device(): lax.dot_general(features, embed, (((1,), (1,)), ((), ())), preferred_elem...  21.8 us
  transfers between devices with their start and end apart: 4, of which 2 were waited for; matrix products, arithmetic and copies ran while one was open for 21% of the time, Pallas kernels for 0%

commit v1 on v0

v1 whole, which is shorter than its diff:
```python
import functools
import math

import jax
import jax.numpy as jnp
from jax import lax
from jax.experimental import pallas as pl
from jax.experimental.pallas import tpu as pltpu
from jax.sharding import PartitionSpec as P

SOFT_CAP = 30.0
LOSS_SCALE = 16.0
TILE = 512
BLOCK = 256
FAST_SLOTS = 4
FAR = 1 << 30


def dot_nn(a, b):
    return lax.dot_general(a, b, (((1,), (0,)), ((), ())), preferred_element_type=jnp.float32)


def dot_nt(a, b):
    return lax.dot_general(a, b, (((1,), (1,)), ((), ())), preferred_element_type=jnp.float32)


def dot_tn(a, b):
    return lax.dot_general(a, b, (((0,), (0,)), ((), ())), preferred_element_type=jnp.float32)


def teacher_kernel(tiles, blocks, place, pack, ids, prob, counts):
    offset = place[0]
    flipped = pack[...].T
    top = flipped.shape[0] // 2
    scores = flipped[:top]
    local = flipped[top:].astype(jnp.int32) - offset
    raised = jnp.exp(scores - jnp.max(scores, axis=0, keepdims=True))
    ids[...] = local
    prob[...] = raised / jnp.sum(raised, axis=0, keepdims=True)
    for tile in range(tiles):
        low = tile * TILE
        inside = ((local >= low) & (local < low + TILE)).astype(jnp.int32)
        held = jnp.sum(inside, axis=0, keepdims=True)
        for block in range(blocks):
            counts[tile * blocks + block] = jnp.max(held[:, block * BLOCK : (block + 1) * BLOCK])


def lookup_kernel(rows, place, tokens, cot, packed_cot, packed_ids, chunks):
    offset = place[0]
    count = tokens.shape[1]
    blocks = count // BLOCK
    local = tokens[...] - offset
    inside = (local >= 0) & (local < rows)
    hit = jnp.broadcast_to(jnp.where(inside, 1.0, 0.0), (8, count))
    before = lax.broadcasted_iota(jnp.int32, (count, count), 0)
    after = lax.broadcasted_iota(jnp.int32, (count, count), 1)
    upto = jnp.where(before <= after, 1.0, 0.0).astype(jnp.bfloat16)
    running = dot_nn(hit.astype(jnp.bfloat16), upto)[0:1].astype(jnp.int32)
    rank = jnp.where(inside, running - 1, -1)
    total = jnp.max(running)
    chunks[0] = (total + BLOCK - 1) // BLOCK
    safe = jnp.where(inside, local, 0)
    high = jnp.broadcast_to((safe >> 6).astype(jnp.float32), (8, count)).astype(jnp.bfloat16)
    low = jnp.broadcast_to((safe & 63).astype(jnp.float32), (8, count)).astype(jnp.bfloat16)
    for chunk in range(blocks):

        @pl.when(chunk * BLOCK < total)
        def _():
            slot = lax.broadcasted_iota(jnp.int32, (BLOCK, count), 0) + chunk * BLOCK
            chosen = jnp.where(slot == rank, 1.0, 0.0).astype(jnp.bfloat16)
            taken = jnp.zeros((cot.shape[1], BLOCK), jnp.float32)
            for block in range(blocks):
                span = slice(block * BLOCK, (block + 1) * BLOCK)
                taken = taken + dot_nt(cot[block], chosen[:, span])
            packed_cot[chunk] = taken.astype(jnp.bfloat16)
            row = dot_nt(high, chosen)[0:1] * 64.0 + dot_nt(low, chosen)[0:1]
            used = dot_nt(hit.astype(jnp.bfloat16), chosen)[0:1] > 0.5
            packed_ids[chunk] = jnp.where(used, row.astype(jnp.int32), -1)


def next_slot(relative, prob, last):
    following = jnp.min(jnp.where(relative > last, relative, FAR), axis=0, keepdims=True)
    chance = jnp.sum(jnp.where(relative == following, prob, 0.0), axis=0, keepdims=True)
    return following, chance


def logit_kernel(blocks, rows, place, counts, embed, hidden, ids, prob, squashed, sums):
    step = pl.program_id(0)
    last_step = pl.num_programs(0) - 1
    mine = place[1]

    @pl.when(step == 0)
    def _():
        sums[...] = jnp.zeros_like(sums)

    def work(size):
        table = embed[0:size]
        for block in range(blocks):
            span = slice(block * BLOCK, (block + 1) * BLOCK)
            raw = dot_nn(table, hidden[block])
            ratio = jnp.tanh(raw * (1.0 / SOFT_CAP))
            squashed[0:size, span] = ratio
            raised = jnp.exp(ratio * SOFT_CAP)
            sums[0:8, span] += jnp.sum(raised.reshape(size // 8, 8, BLOCK), axis=0)
        own = pl.ds(pl.multiple_of(mine * BLOCK, BLOCK), BLOCK)
        row = lax.broadcasted_iota(jnp.int32, (size, BLOCK), 0)

        def pick(_, last):
            relative = ids[:, own] - step * TILE
            following, chance = next_slot(relative, prob[:, own], last)
            found = jnp.where(row == following, squashed[0:size, own], 0.0)
            sums[8:16, 0:BLOCK] += jnp.sum(found.reshape(size // 8, 8, BLOCK), axis=0) * (
                chance * SOFT_CAP
            )
            return following

        lax.fori_loop(0, counts[step * blocks + mine], pick, jnp.full((1, BLOCK), -1, jnp.int32))

    tail = rows - (rows - 1) // TILE * TILE

    @pl.when(step < last_step)
    def _():
        work(TILE)

    @pl.when(step == last_step)
    def _():
        work(tail)


def grad_kernel(
    blocks,
    rows,
    place,
    counts,
    chunks,
    embed,
    squashed,
    inverse,
    ids,
    prob,
    hidden,
    packed_cot,
    packed_ids,
    embed_grad,
    hidden_grad,
    grads,
    total_grad,
):
    step = pl.program_id(0)
    last_step = pl.num_programs(0) - 1
    mine = place[1]
    width = embed.shape[1]

    @pl.when(step == 0)
    def _():
        total_grad[...] = jnp.zeros_like(total_grad)

    def work(size):
        row = lax.broadcasted_iota(jnp.int32, (size, BLOCK), 0)
        for block in range(blocks):
            span = slice(block * BLOCK, (block + 1) * BLOCK)
            relative = ids[:, span] - step * TILE
            chances = prob[:, span]
            last = jnp.full((1, BLOCK), -1, jnp.int32)
            target = jnp.zeros((size, BLOCK), jnp.float32)
            for _ in range(FAST_SLOTS):
                last, chance = next_slot(relative, chances, last)
                target = jnp.where(row == last, chance * LOSS_SCALE, target)
            ratio = squashed[0:size, span]
            share = jnp.exp(ratio * SOFT_CAP) * inverse[:, span]
            grads[block, 0:size] = ((share - target) * (1.0 - ratio * ratio)).astype(jnp.bfloat16)

            def more(_, last):
                last, chance = next_slot(ids[:, span] - step * TILE, prob[:, span], last)
                ratio = squashed[0:size, span]
                share = jnp.exp(ratio * SOFT_CAP) * inverse[:, span]
                fresh = (share - chance * LOSS_SCALE) * (1.0 - ratio * ratio)
                held = grads[block, 0:size].astype(jnp.float32)
                grads[block, 0:size] = jnp.where(row == last, fresh, held).astype(jnp.bfloat16)
                return last

            lax.fori_loop(FAST_SLOTS, counts[step * blocks + block], more, last)

        spread = jnp.zeros((hidden.shape[1], size), jnp.float32)
        for block in range(blocks):
            spread = spread + dot_nt(hidden[block], grads[block, 0:size])
        embed_grad[:, 0:size] = spread.astype(jnp.bfloat16)

        def lookup(chunk, _):
            column = lax.broadcasted_iota(jnp.int32, (size, BLOCK), 0) + step * TILE
            onehot = jnp.where(column == packed_ids[chunk], math.sqrt(width), 0.0)
            return _ + dot_nt(packed_cot[chunk], onehot.astype(jnp.bfloat16))

        spread = lax.fori_loop(0, chunks[0], lookup, spread)
        embed_grad[:, 0:size] = spread.astype(jnp.bfloat16)
        total_grad[...] += dot_tn(grads[mine, 0:size], embed[0:size])

    tail = rows - (rows - 1) // TILE * TILE

    @pl.when(step < last_step)
    def _():
        work(TILE)

    @pl.when(step == last_step)
    def _():
        work(tail)
        hidden_grad[...] = total_grad[...].T


def smem():
    return pl.BlockSpec(memory_space=pltpu.SMEM)


def whole(shape):
    return pl.BlockSpec(shape, lambda *_: (0,) * len(shape))


def per_device(hidden, embed, token_ids, lookup_cot, teacher_ids, teacher_logits):
    rows, width = embed.shape
    dp = lax.axis_size("dp")
    vocab = lax.axis_size("vocab")
    dp_index = lax.axis_index("dp")
    vocab_index = lax.axis_index("vocab")
    here = hidden.shape[0]
    thin = hidden.shape[1]
    tokens = here * dp
    top = teacher_ids.shape[1]
    tiles = pl.cdiv(rows, TILE)
    share = here // vocab
    columns = width // dp
    both = ("dp", "vocab")
    place = jnp.stack([vocab_index * rows, dp_index]).astype(jnp.int32)

    pack = lax.all_gather(
        jnp.concatenate([teacher_logits, teacher_ids.astype(jnp.float32)], axis=1),
        both,
        axis=0,
        tiled=True,
    )
    hidden_all = lax.all_gather(hidden.T, both, axis=0, tiled=True).reshape(dp, width, here)
    token_all = lax.all_gather(token_ids, "dp", axis=0, tiled=True).reshape(1, tokens)
    per = vocab // dp
    route = [
        (i * vocab + j, (j // per) * vocab + i * per + j % per)
        for i in range(dp)
        for j in range(vocab)
    ]
    moved = lax.ppermute(lookup_cot.T, both, route)
    cot = lax.all_gather(moved, "vocab", axis=0, tiled=True).reshape(dp, columns, here)

    ids, prob, counts = pl.pallas_call(
        functools.partial(teacher_kernel, tiles, dp),
        out_shape=(
            jax.ShapeDtypeStruct((top, tokens), jnp.int32),
            jax.ShapeDtypeStruct((top, tokens), jnp.float32),
            jax.ShapeDtypeStruct((tiles * dp,), jnp.int32),
        ),
        in_specs=[smem(), pl.BlockSpec(memory_space=pltpu.VMEM)],
        out_specs=(
            pl.BlockSpec(memory_space=pltpu.VMEM),
            pl.BlockSpec(memory_space=pltpu.VMEM),
            smem(),
        ),
        name="teacher_prep",
    )(place, pack)

    squashed, sums = pl.pallas_call(
        functools.partial(logit_kernel, dp, rows),
        grid=(tiles,),
        in_specs=[
            smem(),
            smem(),
            pl.BlockSpec((TILE, width), lambda n: (n, 0)),
            whole((dp, width, here)),
            whole((top, tokens)),
            whole((top, tokens)),
        ],
        out_specs=(
            pl.BlockSpec((TILE, tokens), lambda n: (n, 0)),
            whole((16, tokens)),
        ),
        out_shape=(
            jax.ShapeDtypeStruct((rows, tokens), jnp.float32),
            jax.ShapeDtypeStruct((16, tokens), jnp.float32),
        ),
        compiler_params=pltpu.CompilerParams(vmem_limit_bytes=40 << 20),
        cost_estimate=pl.CostEstimate(
            flops=2 * rows * width * tokens,
            bytes_accessed=rows * width * 2 + rows * tokens * 4,
            transcendentals=2 * rows * tokens,
        ),
        name="logits",
    )(place, counts, embed, hidden_all, ids, prob)

    packed_cot, packed_ids, chunks = pl.pallas_call(
        functools.partial(lookup_kernel, rows),
        out_shape=(
            jax.ShapeDtypeStruct((dp, columns, here), jnp.bfloat16),
            jax.ShapeDtypeStruct((dp, 1, here), jnp.int32),
            jax.ShapeDtypeStruct((1,), jnp.int32),
        ),
        in_specs=[
            smem(),
            pl.BlockSpec(memory_space=pltpu.VMEM),
            pl.BlockSpec(memory_space=pltpu.VMEM),
        ],
        out_specs=(
            pl.BlockSpec(memory_space=pltpu.VMEM),
            pl.BlockSpec(memory_space=pltpu.VMEM),
            smem(),
        ),
        name="lookup_prep",
    )(place, token_all, cot)

    parts = jnp.concatenate(
        [jnp.sum(sums[0:8], axis=0), jnp.sum(sums[8:16, 0:here], axis=0)], axis=0
    )
    sums_all = lax.psum(parts, "vocab")
    total = sums_all[0:tokens]
    term = sums_all[tokens:]
    inverse = (LOSS_SCALE / total).reshape(1, tokens)

    embed_grad, hidden_part = pl.pallas_call(
        functools.partial(grad_kernel, dp, rows),
        grid_spec=pltpu.PrefetchScalarGridSpec(
            num_scalar_prefetch=3,
            grid=(tiles,),
            in_specs=[
                pl.BlockSpec((TILE, width), lambda n, *_: (n, 0)),
                pl.BlockSpec((TILE, tokens), lambda n, *_: (n, 0)),
                whole((1, tokens)),
                whole((top, tokens)),
                whole((top, tokens)),
                pl.BlockSpec((dp, columns, here), lambda n, place, *_: (0, place[1], 0)),
                whole((dp, columns, here)),
                whole((dp, 1, here)),
            ],
            out_specs=[
                pl.BlockSpec((columns, TILE), lambda n, *_: (0, n)),
                whole((width, here)),
            ],
            scratch_shapes=[
                pltpu.VMEM((dp, TILE, here), jnp.bfloat16),
                pltpu.VMEM((here, width), jnp.float32),
            ],
        ),
        out_shape=(
            jax.ShapeDtypeStruct((columns, rows), jnp.bfloat16),
            jax.ShapeDtypeStruct((width, here), jnp.float32),
        ),
        compiler_params=pltpu.CompilerParams(vmem_limit_bytes=48 << 20),
        cost_estimate=pl.CostEstimate(
            flops=4 * rows * width * here,
            bytes_accessed=rows * width * 2 + rows * tokens * 4 + rows * columns * 2,
            transcendentals=rows * tokens,
        ),
        name="grads",
    )(place, counts, chunks, embed, squashed, inverse, ids, prob, hidden_all, packed_cot, packed_ids)

    summed = lax.psum_scatter(hidden_part, "vocab", scatter_dimension=0, tiled=True)
    hidden_grad = summed.astype(jnp.bfloat16).T

    own_prob = jax.nn.softmax(teacher_logits, axis=1)
    first = vocab_index * share
    own_total = lax.dynamic_slice_in_dim(total, dp_index * here + first, share, 0)
    own_term = lax.dynamic_slice_in_dim(term, first, share, 0)
    divergence = (
        jnp.sum(own_prob * jnp.log(own_prob), axis=1) - own_term + jnp.log(own_total)
    )
    return (hidden_grad, embed_grad.T, divergence)


def solution(mesh):
    placed = (
        P("dp", "vocab"),
        P("vocab", None),
        P("dp"),
        P("dp", "vocab"),
        P(("dp", "vocab"), None),
        P(("dp", "vocab"), None),
    )
    return jax.shard_map(
        per_device,
        mesh=mesh,
        in_specs=placed,
        out_specs=(P("dp", "vocab"), P("vocab", "dp"), P(("dp", "vocab"))),
        check_vma=False,
    )
```

time: 632 us -> 355 us (0.56); the launches traced: 622 us -> 354 us
  waiting for transfers between devices: 353 us -> 128 us
  Pallas kernels: 0 us -> 74.2 us
  matrix products: 72.2 us -> 0 us
  other arithmetic: 59.3 us -> 4.73 us
  blocking collectives: 116 us -> 125 us
    reduce_scatter x1, waiting for transfers between devices: 317 us -> 73.1 us  [per_device(): lax.psum_scatter(hidden_part, 'vocab', scatter_dimension=0, tiled=True)]
    pallas_call x0 -> x4, Pallas kernels: none -> 74.2 us  [the longest x1 40.1 us: per_device(): pl.pallas_call(functools.partial(grad_kernel, dp, rows), grid_spec=pltpu....]
    dot_general x4 -> x0, matrix products: 72.2 us -> none  [the longest x1 24.8 us: per_device(): lax.dot_general(onehot, cot_full, (((0,), (0,)), ((), ())), preferred_ele...]
    all_gather x2, waiting for transfers between devices: 0.01 us -> 54.6 us  [the longest x1 54.6 us: per_device(): lax.all_gather(hidden.T, both, axis=0, tiled=True).reshape(dp, width, here)]
    reduce_sum x6 -> x4, other arithmetic: 47.9 us -> 0.41 us  [the longest x1 0.2 us: per_device(): jnp.sum(own_prob * jnp.log(own_prob), axis=1) - own_term]
    unnamed x5 -> x3, waiting for transfers between devices: 36.5 us -> 0.73 us
    convert_element_type x2 -> x1, other arithmetic: 11.2 us -> 0.69 us  [per_device(): teacher_ids.astype(jnp.float32)]
    all_gather x2, blocking collectives: 50.2 us -> 58.6 us  [the longest x1 49.3 us: per_device(): lax.all_gather(jnp.concatenate([teacher_logits, teacher_ids.astype(jnp.fl...]
  transfers between devices with their start and end apart: 4 -> 4, of which waited for: 2 -> 2; matrix products, arithmetic and copies ran while one was open for 21% -> 1% of each run, Pallas kernels for 0% -> 2%
where the time goes in v1:
time: 355 us; the launch traced here: 354 us
  waiting for transfers between devices  128 us (36%)
  blocking collectives  125 us (35%)
  Pallas kernels  74.2 us (21%)
  between operations  13.9 us (4%)
  local copies, waits for them, and re-layouts  6.15 us (2%)
  other arithmetic  4.73 us (1%)
    reduce_scatter x1, waiting for transfers between devices, per_device(): lax.psum_scatter(hidden_part, 'vocab', scatter_dimension=0, tiled=True)  73.1 us
    psum x1, blocking collectives, per_device(): sums_all = lax.psum(parts, 'vocab')  66.4 us
    all_gather x1, waiting for transfers between devices, per_device(): lax.all_gather(hidden.T, both, axis=0, tiled=True).reshape(dp, width, here)  54.6 us
    all_gather x1, blocking collectives, per_device(): lax.all_gather(jnp.concatenate([teacher_logits, teacher_ids.astype(jnp.fl...  49.3 us
    pallas_call x1, Pallas kernels, per_device(): pl.pallas_call(functools.partial(grad_kernel, dp, rows), grid_spec=pltpu....  40.1 us
    pallas_call x1, Pallas kernels, per_device(): pl.pallas_call(functools.partial(logit_kernel, dp, rows), grid=(tiles,),...  28 us
    all_gather x1, blocking collectives, per_device(): lax.all_gather(token_ids, 'dp', axis=0, tiled=True).reshape(1, tokens)  9.29 us
  transfers between devices with their start and end apart: 4, of which 2 were waited for; matrix products, arithmetic and copies ran while one was open for 1% of the time, Pallas kernels for 2%

profile of v1, /device:TPU:0, one launch (start us, length us, event | category | flops | bytes accessed | tf_op | source)
XLA Modules:
  0.0 353.9 jit_solution(12288100448664702846)
XLA Ops:
  7.2 0.0 all-gather.4.cloned.1.call-start
  7.2 1.4 collective-permute-start
  8.6 0.6 copy-done.12
  9.3 0.0 all-gather.4.cloned.1.call-update
  9.3 0.0 all-gather.6.cloned.1.call-start
  9.3 0.7 all-gather.6.cloned.1.call-update
  10.0 0.0 reduce-scatter.2.cloned.1.call-start
  10.1 0.7 convert_element_type.6
  10.8 0.6 pad_add_fusion.place
  11.4 0.8 pad_maximum_fusion.1
  12.2 49.3 %all_gather.12.pack = f32[1024,128]{1,0:T(8,128)} all-gather(f32[8,128]{1,0:T(8,128)S(1)} %pad_maximum_fusion.1), channel_id=1, replica_groups=mesh['dp'=4,'vocab'=32] {'dp','vocab'}, dimensions={0}, use_global_device_ids=true | all-gather | bytes 528384 | tf_op jit(solution)/shard_map/all_gather | solution.py:234
  61.5 2.3 teacher_prep.1
  63.8 9.3 %all-gather = s32[4,1,256]{2,1,0:T(1,128)} all-gather(s32[1,1,256]{2,1,0:T(1,128)} %bitcast.18), channel_id=1, replica_groups=mesh['dp'=4,'vocab'=32] {'dp'}, dimensions={0}, use_global_device_ids=true | all-gather | bytes 5120 | tf_op jit(solution)/shard_map/all_gather | solution.py:241
  73.1 3.7 %lookup_prep.1 = (bf16[4,576,256]{2,1,0:T(8,128)(2,1)}, s32[4,1,256]{2,1,0:T(1,128)}, s32[1]{0:T(128)}) custom-call(s32[2]{0:T(128)} %pad_add_fusion.place, s32[1,1024]{1,0:T(1,128)} %bitcast.17, bf16[4,576,256]{2,1,0:T(8,128)(2,1)} %bitcast.15), custom_call_target="tpu_custom_call" | custom-call | tf_op jit(solution)/shard_map/lookup_prep/pallas_call | solution.py:295
  76.8 54.6 %all-gather.6.cloned.1.call-done = bf16[9216,256]{1,0:T(8,128)(2,1)} async-done(((bf16[72,256]{1,0:T(8,128)(2,1)}), bf16[9216,256]{1,0:T(8,128)(2,1)}) %all-gather.6.cloned.1.call-update) | async-done | bytes 4718608 | tf_op jit(solution)/shard_map/all_gather | solution.py:240
  131.4 2.3 copy-done
  133.8 0.9 copy-done.2
  134.7 0.9 copy-done.4
  135.7 0.7 copy-done.6
  136.3 0.6 copy-done.9
  136.9 0.0 copy-start.8
  137.0 28.0 %logits.1 = (f32[4000,1024]{1,0:T(8,128)}, f32[16,1024]{1,0:T(8,128)S(1)}) custom-call(s32[2]{0:T(128)S(1)} %copy-done.6, s32[32]{0:T(128)S(1)} %copy-done.9, bf16[4000,2304]{1,0:T(8,128)(2,1)} %embed.3, bf16[4,2304,256]{2,1,0:T(8,128)(2,1)S(1)} %bitcast.13, s32[64,1024]{1,0:T(8,128)S(1)} %copy-done.2, f32[64,1024]{1,0:T(8,128)S(1)} %copy-done.4), custom_call_target="tpu_custom_call" | custom-call | flops 18874368000 | bytes 34816000 | tf_op jit(solution)/shard_map/logits/pallas_call | solution.py:267
  165.0 66.4 %psum.7 = f32[1280]{0:T(1024)S(1)} all-reduce(f32[1280]{0:T(1024)S(1)} %pad_maximum_fusion), channel_id=1, replica_groups=mesh['dp'=4,'vocab'=32] {'vocab'}, use_global_device_ids=true, to_apply=%region_2.0 | all-reduce | flops 1280 | bytes 10240 | tf_op jit(solution)/shard_map/psum | solution.py:318
  231.5 0.0 copy-start.11
  231.5 40.1 %grads.1 = (bf16[576,4000]{1,0:T(8,128)(2,1)}, f32[2304,256]{1,0:T(8,128)}) custom-call(s32[2]{0:T(128)S(1)} %copy-done.7, s32[32]{0:T(128)S(1)} %copy-done.10, s32[1]{0:T(128)} %get-tuple-element.14.chunks, bf16[4000,2304]{1,0:T(8,128)(2,1)} %embed.3, f32[4000,1024]{1,0:T(8,128)} %get-tuple-element.17.squashed, f32[1,1024]{1,0:T(1,128)S(1)} %bitcast.14, ...), custom_call_target="tpu_custom_call" | custom-call | flops 9437184000 | bytes 39424000 | tf_op jit(solution)/shard_map/grads/pallas_call | solution.py:323
  271.6 0.0 reduce-scatter.2.cloned.1.call-update
  271.7 0.1 reduce_max.9
  271.8 0.2 fusion.1
  272.0 0.2 fusion
  272.2 0.6 log_add_fusion
  272.8 73.1 %reduce-scatter.2.cloned.1.call-done = f32[72,256]{1,0:T(8,128)} async-done(((f32[2304,256]{1,0:T(8,128)}), f32[72,256]{1,0:T(8,128)}) %reduce-scatter.2.cloned.1.call-update) | async-done | bytes 73744 | tf_op jit(solution)/shard_map/reduce_scatter | solution.py:360
  345.9 1.5 convert_bitcast_fusion
  (25 shorter events, 0.1 us)
Async XLA Ops:
  7.2 65.9 %all-gather.4.cloned.1.call-start = ((), (), s32[]{:S(2)}) async-start(), calls=%async_computation.1 | async-start | bytes 1216512 | tf_op jit(solution)/shard_map/all_gather | solution.py:249
  7.2 1.4 collective-permute-start
  8.6 0.6 copy-start.12
  9.3 122.1 %all-gather.6.cloned.1.call-start = ((), (), s32[]{:S(2)}) async-start(), calls=%async_computation.2 | async-start | bytes 4755456 | tf_op jit(solution)/shard_map/all_gather | solution.py:240
  10.0 335.8 %reduce-scatter.2.cloned.1.call-start = ((), (), s32[]{:S(2)}) async-start(), calls=%async_computation.3 | async-start | bytes 2433024 | tf_op jit(solution)/shard_map/reduce_scatter | solution.py:360
  131.4 2.3 copy-start
  133.8 0.9 copy-start.2
  134.7 0.9 copy-start.4
  135.7 0.7 copy-start.6
  136.3 0.6 copy-start.9
  136.9 94.5 %copy-start.1 = (bf16[4,576,256]{2,1,0:T(8,128)(2,1)S(1)}, bf16[4,576,256]{2,1,0:T(8,128)(2,1)}, u32[]{:S(2)}) copy-start(bf16[4,576,256]{2,1,0:T(8,128)(2,1)} %get-tuple-element.19.packed_cot) | copy-start | bytes 3538948
  136.9 94.5 %copy-start.3 = (s32[64,1024]{1,0:T(8,128)S(1)}, s32[64,1024]{1,0:T(8,128)}, u32[]{:S(2)}) copy-start(s32[64,1024]{1,0:T(8,128)} %get-tuple-element.15.ids) | copy-start | bytes 786436
  136.9 94.5 %copy-start.5 = (f32[64,1024]{1,0:T(8,128)S(1)}, f32[64,1024]{1,0:T(8,128)}, u32[]{:S(2)}) copy-start(f32[64,1024]{1,0:T(8,128)} %get-tuple-element.16.prob) | copy-start | bytes 786436
  136.9 94.5 %copy-start.7 = (s32[2]{0:T(128)S(1)}, s32[2]{0:T(128)}, u32[]{:S(2)}) copy-start(s32[2]{0:T(128)} %pad_add_fusion.place) | copy-start | bytes 28
  136.9 94.5 %copy-start.8 = (s32[4,1,256]{2,1,0:T(1,128)S(1)}, s32[4,1,256]{2,1,0:T(1,128)}, u32[]{:S(2)}) copy-start(s32[4,1,256]{2,1,0:T(1,128)} %get-tuple-element.20.packed_ids) | copy-start | bytes 12292
  136.9 94.5 %copy-start.10 = (s32[32]{0:T(128)S(1)}, s32[32]{0:T(128)}, u32[]{:S(2)}) copy-start(s32[32]{0:T(128)} %get-tuple-element.13.counts) | copy-start | bytes 388
  231.5 40.2 %copy-start.11 = (f32[8,64]{1,0:T(8,128)S(1)}, f32[8,64]{1,0:T(8,128)}, u32[]{:S(2)}) copy-start(f32[8,64]{1,0:T(8,128)} %param.11) | copy-start | bytes 6148
Sparse Core Ops, SparseCore 0:
  10.9 51.1 all-gather.3
  65.2 66.1 all-gather.5
  271.8 74.0 reduce-scatter.1

commit v2 on v0

v2 whole, which is shorter than its diff:
```python
import functools
import math

import jax
import jax.numpy as jnp
from jax import lax
from jax.experimental import pallas as pl
from jax.experimental.pallas import tpu as pltpu
from jax.sharding import Mesh, PartitionSpec as P

SOFT_CAP = 30.0
LOSS_SCALE = 16.0
BLOCK = 256
HALF = 128
ROW_TILE = 400
COLUMN_TILE = 512
FAST_SLOTS = 4
FAR = 1 << 30
SHIFTS = (0, 1, 3, 2)
RING = ("z", "y", "core")
PLANE = ("z", "y")


def dot_nn(a, b):
    return lax.dot_general(a, b, (((1,), (0,)), ((), ())), preferred_element_type=jnp.float32)


def dot_nt(a, b):
    return lax.dot_general(a, b, (((1,), (1,)), ((), ())), preferred_element_type=jnp.float32)


def dot_tn(a, b):
    return lax.dot_general(a, b, (((0,), (0,)), ((), ())), preferred_element_type=jnp.float32)


def teacher_kernel(rows, place, pack, ids, prob, row_counts, column_counts):
    offset = place[0]
    mine = place[1]
    blocks = pack.shape[1]
    top = pack.shape[3] // 2
    for block in range(blocks):
        source = lax.rem(mine + SHIFTS[block], blocks)
        flipped = pack[:, source].reshape(BLOCK, 2 * top).T
        scores = flipped[:top]
        local = flipped[top:].astype(jnp.int32) - offset
        raised = jnp.exp(scores - jnp.max(scores, axis=0, keepdims=True))
        ids[block] = local
        prob[block] = raised / jnp.sum(raised, axis=0, keepdims=True)
        size, held = (ROW_TILE, row_counts) if block == 0 else (COLUMN_TILE, column_counts)
        for tile in range(pl.cdiv(rows, size)):
            inside = (local >= tile * size) & (local < tile * size + size)
            most = jnp.max(jnp.sum(inside.astype(jnp.int32), axis=0))
            if block == 0:
                held[tile] = most
            else:
                held[tile * (blocks - 1) + block - 1] = most


def lookup_kernel(rows, place, tokens, cot, packed_cot, packed_ids, chunks):
    offset = place[0]
    count = tokens.shape[1]
    blocks = count // BLOCK
    local = tokens[...] - offset
    inside = (local >= 0) & (local < rows)
    hit = jnp.broadcast_to(jnp.where(inside, 1.0, 0.0), (8, count))
    before = lax.broadcasted_iota(jnp.int32, (count, count), 0)
    after = lax.broadcasted_iota(jnp.int32, (count, count), 1)
    upto = jnp.where(before <= after, 1.0, 0.0).astype(jnp.bfloat16)
    running = dot_nn(hit.astype(jnp.bfloat16), upto)[0:1].astype(jnp.int32)
    rank = jnp.where(inside, running - 1, -1)
    total = jnp.max(running)
    chunks[0] = (total + BLOCK - 1) // BLOCK
    safe = jnp.where(inside, local, 0)
    high = jnp.broadcast_to((safe >> 6).astype(jnp.float32), (8, count)).astype(jnp.bfloat16)
    low = jnp.broadcast_to((safe & 63).astype(jnp.float32), (8, count)).astype(jnp.bfloat16)
    for chunk in range(blocks):

        @pl.when(chunk * BLOCK < total)
        def _():
            slot = lax.broadcasted_iota(jnp.int32, (BLOCK, count), 0) + chunk * BLOCK
            chosen = jnp.where(slot == rank, 1.0, 0.0).astype(jnp.bfloat16)
            taken = jnp.zeros((cot.shape[1], BLOCK), jnp.float32)
            for block in range(blocks):
                span = slice(block * BLOCK, (block + 1) * BLOCK)
                taken = taken + dot_nt(cot[block], chosen[:, span])
            packed_cot[chunk] = taken.astype(jnp.bfloat16)
            row = dot_nt(high, chosen)[0:1] * 64.0 + dot_nt(low, chosen)[0:1]
            used = dot_nt(hit.astype(jnp.bfloat16), chosen)[0:1] > 0.5
            packed_ids[chunk] = jnp.where(used, row.astype(jnp.int32), -1)


def next_slot(relative, prob, last):
    following = jnp.min(jnp.where(relative > last, relative, FAR), axis=0, keepdims=True)
    chance = jnp.sum(jnp.where(relative == following, prob, 0.0), axis=0, keepdims=True)
    return following, chance


def join_halves(core, near, far, joined):
    joined[:, pl.ds(pl.multiple_of(core * HALF, HALF), HALF)] = near
    joined[:, pl.ds(pl.multiple_of((1 - core) * HALF, HALF), HALF)] = far


def logit_kernel(blocks, place, embed, *refs):
    near, far = refs[:blocks], refs[blocks : 2 * blocks]
    squashed, total, hidden, sums = refs[2 * blocks :]
    step = pl.program_id(0)
    size = embed.shape[0]

    @pl.when(step == 0)
    def _():
        sums[...] = jnp.zeros_like(sums)
        for block in range(blocks):
            join_halves(place[2], near[block][...], far[block][...], hidden.at[block])

    table = embed[...]
    for block in range(blocks):
        span = slice(block * BLOCK, (block + 1) * BLOCK)
        raw = dot_nn(table, hidden[block])
        ratio = jnp.tanh(raw * (1.0 / SOFT_CAP))
        squashed[:, span] = ratio
        raised = jnp.exp(ratio * SOFT_CAP)
        sums[:, span] += jnp.sum(raised.reshape(size // 8, 8, BLOCK), axis=0)

    @pl.when(step == pl.num_programs(0) - 1)
    def _():
        total[...] = jnp.sum(sums[...], axis=0, keepdims=True)


def place_targets(relative, chances, row):
    last = jnp.full((1, BLOCK), -1, jnp.int32)
    target = jnp.zeros(row.shape, jnp.float32)
    for _ in range(FAST_SLOTS):
        last, chance = next_slot(relative, chances, last)
        target = jnp.where(row == last, chance * LOSS_SCALE, target)
    return target, last


def hidden_grad_kernel(
    place, counts, embed, squashed, parts, ids, prob, grads, keep, give, rows_grad, flipped, term
):
    step = pl.program_id(0)
    size, width = embed.shape
    inverse = LOSS_SCALE / jnp.sum(parts[:, :, 0:BLOCK], axis=0)

    @pl.when(step == 0)
    def _():
        rows_grad[...] = jnp.zeros_like(rows_grad)
        term[...] = jnp.zeros_like(term)

    row = lax.broadcasted_iota(jnp.int32, (size, BLOCK), 0)
    target, last = place_targets(ids[0] - step * size, prob[0], row)
    ratio = squashed[...]
    share = jnp.exp(ratio * SOFT_CAP) * inverse
    grads[...] = ((share - target) * (1.0 - ratio * ratio)).astype(jnp.bfloat16)
    term[...] += jnp.sum((target * ratio).reshape(size // 8, 8, BLOCK), axis=0)

    def more(_, last):
        last, chance = next_slot(ids[0] - step * size, prob[0], last)
        ratio = squashed[...]
        share = jnp.exp(ratio * SOFT_CAP) * inverse
        target = jnp.where(row == last, chance * LOSS_SCALE, 0.0)
        fresh = (share - target) * (1.0 - ratio * ratio)
        held = grads[...].astype(jnp.float32)
        grads[...] = jnp.where(row == last, fresh, held).astype(jnp.bfloat16)
        term[...] += jnp.sum((target * ratio).reshape(size // 8, 8, BLOCK), axis=0)
        return last

    lax.fori_loop(FAST_SLOTS, counts[step], more, last)
    rows_grad[...] += dot_tn(grads[...], embed[...])

    @pl.when(step == pl.num_programs(0) - 1)
    def _():
        core = place[2]
        thin = keep.shape[1] - 8
        for part in range(width // BLOCK):
            span = slice(part * BLOCK, (part + 1) * BLOCK)
            flipped[span, :] = rows_grad[:, span].T
        total = jnp.sum(term[...], axis=0, keepdims=True) * (SOFT_CAP / LOSS_SCALE)
        for chip in range(keep.shape[0]):
            for ref, side in ((keep, core), (give, 1 - core)):
                start = pl.multiple_of((2 * chip + side) * thin, 8)
                ref[chip, 0:thin] = flipped[pl.ds(start, thin)]
                ref[chip, thin : thin + 8] = jnp.broadcast_to(total, (8, BLOCK))


def table_grad_kernel(
    rows,
    width,
    place,
    counts,
    chunks,
    own_grads,
    side_squashed,
    far_squashed,
    side_parts,
    far_parts,
    ids,
    prob,
    packed_cot,
    packed_ids,
    *refs,
):
    blocks = len(SHIFTS)
    near, far = refs[:blocks], refs[blocks : 2 * blocks]
    embed_grad, hidden, grads, inverse = refs[2 * blocks :]
    step = pl.program_id(0)
    last_step = pl.num_programs(0) - 1

    @pl.when(step == 0)
    def _():
        for block in range(blocks):
            join_halves(place[2], near[block][...], far[block][...], hidden.at[block])
        side = LOSS_SCALE / jnp.sum(side_parts[...], axis=0)
        inverse[0] = side[:, BLOCK : 2 * BLOCK]
        inverse[1] = side[:, 2 * BLOCK : 3 * BLOCK]
        inverse[2] = LOSS_SCALE / jnp.sum(far_parts[...], axis=0)

    def work(size):
        row = lax.broadcasted_iota(jnp.int32, (size, BLOCK), 0)

        def ratio_of(block):
            if block == 2:
                return far_squashed[0:size]
            return side_squashed[0:size, block * BLOCK : (block + 1) * BLOCK]

        for block in range(blocks - 1):
            relative = ids[block + 1] - step * COLUMN_TILE
            target, last = place_targets(relative, prob[block + 1], row)
            ratio = ratio_of(block)
            share = jnp.exp(ratio * SOFT_CAP) * inverse[block]
            grads[block, 0:size] = ((share - target) * (1.0 - ratio * ratio)).astype(jnp.bfloat16)

            def more(_, last):
                relative = ids[block + 1] - step * COLUMN_TILE
                last, chance = next_slot(relative, prob[block + 1], last)
                ratio = ratio_of(block)
                share = jnp.exp(ratio * SOFT_CAP) * inverse[block]
                fresh = (share - chance * LOSS_SCALE) * (1.0 - ratio * ratio)
                held = grads[block, 0:size].astype(jnp.float32)
                grads[block, 0:size] = jnp.where(row == last, fresh, held).astype(jnp.bfloat16)
                return last

            lax.fori_loop(FAST_SLOTS, counts[step * (blocks - 1) + block], more, last)

        spread = dot_nt(hidden[0], own_grads[0:size])
        for block in range(blocks - 1):
            spread = spread + dot_nt(hidden[block + 1], grads[block, 0:size])

        def lookup(chunk, held):
            column = lax.broadcasted_iota(jnp.int32, (size, BLOCK), 0) + step * COLUMN_TILE
            onehot = jnp.where(column == packed_ids[chunk], math.sqrt(width), 0.0)
            return held + dot_nt(packed_cot[chunk], onehot.astype(jnp.bfloat16))

        spread = lax.fori_loop(0, chunks[0], lookup, spread)
        embed_grad[:, 0:size] = spread.astype(jnp.bfloat16)

    @pl.when(step < last_step)
    def _():
        work(COLUMN_TILE)

    @pl.when(step == last_step)
    def _():
        work(rows - (rows - 1) // COLUMN_TILE * COLUMN_TILE)


def smem():
    return pl.BlockSpec(memory_space=pltpu.SMEM)


def vmem():
    return pl.BlockSpec(memory_space=pltpu.VMEM)


def whole(shape):
    return pl.BlockSpec(shape, lambda *_: (0,) * len(shape))


def shape_of(shape, dtype):
    return jax.ShapeDtypeStruct(shape, dtype)


def logits_call(place, embed, near, far):
    blocks = len(near)
    rows, width = embed.shape
    tokens = blocks * BLOCK
    return pl.pallas_call(
        functools.partial(logit_kernel, blocks),
        grid=(rows // ROW_TILE,),
        in_specs=[smem(), pl.BlockSpec((ROW_TILE, width), lambda n: (n, 0))]
        + [whole((width, HALF))] * (2 * blocks),
        out_specs=(pl.BlockSpec((ROW_TILE, tokens), lambda n: (n, 0)), whole((1, tokens))),
        out_shape=(shape_of((rows, tokens), jnp.float32), shape_of((1, tokens), jnp.float32)),
        scratch_shapes=[
            pltpu.VMEM((blocks, width, BLOCK), jnp.bfloat16),
            pltpu.VMEM((8, tokens), jnp.float32),
        ],
        compiler_params=pltpu.CompilerParams(vmem_limit_bytes=36 << 20),
        cost_estimate=pl.CostEstimate(
            flops=2 * rows * width * tokens,
            bytes_accessed=rows * width * 2 + rows * tokens * 4,
            transcendentals=2 * rows * tokens,
        ),
        name=f"logits_{blocks}",
    )(place, embed, *near, *far)


def spread_to(value, axes):
    count = lax.axis_size(axes)
    copies = jnp.broadcast_to(value[None], (count,) + value.shape)
    return lax.all_to_all(copies, axes, 0, 0, tiled=True)


def swap(value):
    return lax.ppermute(value, "core", [(0, 1), (1, 0)])


def shift(value, by):
    count = lax.axis_size("dp")
    return lax.ppermute(value, "dp", [(k, (k + by) % count) for k in range(count)])


def per_device(hidden, embed, token_ids, lookup_cot, teacher_ids, teacher_logits):
    rows, width = embed.shape
    dp = lax.axis_size("dp")
    vocab = lax.axis_size(RING)
    mine = lax.axis_index("dp")
    core = lax.axis_index("core")
    vocab_index = lax.axis_index(RING)
    here, thin = hidden.shape
    tokens = here * dp
    top = teacher_ids.shape[1]
    share = here // vocab
    columns = width // dp
    chips = vocab // 2
    blocks = len(SHIFTS)
    place = jnp.stack([vocab_index * rows, mine, core]).astype(jnp.int32)

    flat = hidden.T
    low, high = flat[:, :HALF], flat[:, HALF:]
    got = swap(jnp.where(core == 0, high, low))
    kept = jnp.where(core == 0, low, high)
    pair = jnp.where(
        core == 0, jnp.concatenate([kept, got], 0), jnp.concatenate([got, kept], 0)
    )
    own_near = spread_to(pair, PLANE).reshape(width, HALF)
    previous_near = shift(own_near, 1)
    next_near = shift(own_near, -1)
    own_far = swap(own_near)
    own_squashed, own_total = logits_call(place, embed, [own_near], [own_far])
    middle = width // 2
    far_upper = shift(previous_near[:middle], 1)
    far_lower = shift(next_near[middle:], -1)
    next_far = swap(next_near)
    previous_far = swap(previous_near)
    side_squashed, side_total = logits_call(
        place, embed, [next_near, previous_near], [next_far, previous_far]
    )
    opposite_near = jnp.concatenate([far_upper, far_lower], axis=0)
    opposite_far = swap(opposite_near)
    side_parts = spread_to(jnp.concatenate([own_total, side_total], axis=1), RING)
    far_squashed, far_total = logits_call(place, embed, [opposite_near], [opposite_far])
    far_parts = spread_to(far_total, RING)

    pack = jnp.concatenate(
        [
            jnp.concatenate([teacher_logits, teacher_ids.astype(jnp.float32)], axis=1),
            token_ids.astype(jnp.float32).reshape(here // HALF, HALF),
            jnp.zeros((8 - here // HALF, HALF), jnp.float32),
        ],
        axis=0,
    )
    pack = spread_to(pack, "dp")
    token_all = pack[:, share : share + here // HALF].reshape(1, tokens).astype(jnp.int32)
    pack = spread_to(pack[:, :share], RING)

    per = vocab // dp
    route = [
        (i * vocab + j, (j // per) * vocab + i * per + j % per)
        for i in range(dp)
        for j in range(vocab)
    ]
    moved = lax.ppermute(lookup_cot.T, ("dp",) + RING, route)
    cot = spread_to(moved, RING).reshape(dp, columns, here)

    row_tiles = rows // ROW_TILE
    column_tiles = pl.cdiv(rows, COLUMN_TILE)
    ids, prob, row_counts, column_counts = pl.pallas_call(
        functools.partial(teacher_kernel, rows),
        out_shape=(
            shape_of((blocks, top, BLOCK), jnp.int32),
            shape_of((blocks, top, BLOCK), jnp.float32),
            shape_of((row_tiles,), jnp.int32),
            shape_of((column_tiles * (blocks - 1),), jnp.int32),
        ),
        in_specs=[smem(), vmem()],
        out_specs=(vmem(), vmem(), smem(), smem()),
        name="teacher_prep",
    )(place, pack)

    packed_cot, packed_ids, chunks = pl.pallas_call(
        functools.partial(lookup_kernel, rows),
        out_shape=(
            shape_of((dp, columns, here), jnp.bfloat16),
            shape_of((dp, 1, here), jnp.int32),
            shape_of((1,), jnp.int32),
        ),
        in_specs=[smem(), vmem(), vmem()],
        out_specs=(vmem(), vmem(), smem()),
        name="lookup_prep",
    )(place, token_all, cot)

    own_grads, keep, give = pl.pallas_call(
        hidden_grad_kernel,
        grid=(row_tiles,),
        in_specs=[
            smem(),
            smem(),
            pl.BlockSpec((ROW_TILE, width), lambda n: (n, 0)),
            pl.BlockSpec((ROW_TILE, BLOCK), lambda n: (n, 0)),
            whole(side_parts.shape),
            whole(ids.shape),
            whole(prob.shape),
        ],
        out_specs=[
            pl.BlockSpec((ROW_TILE, BLOCK), lambda n: (n, 0)),
            whole((chips, thin + 8, BLOCK)),
            whole((chips, thin + 8, BLOCK)),
        ],
        out_shape=(
            shape_of((rows, BLOCK), jnp.bfloat16),
            shape_of((chips, thin + 8, BLOCK), jnp.float32),
            shape_of((chips, thin + 8, BLOCK), jnp.float32),
        ),
        scratch_shapes=[
            pltpu.VMEM((BLOCK, width), jnp.float32),
            pltpu.VMEM((width, BLOCK), jnp.float32),
            pltpu.VMEM((8, BLOCK), jnp.float32),
        ],
        compiler_params=pltpu.CompilerParams(vmem_limit_bytes=36 << 20),
        cost_estimate=pl.CostEstimate(
            flops=2 * rows * width * BLOCK,
            bytes_accessed=rows * width * 2 + rows * BLOCK * 6,
            transcendentals=rows * BLOCK,
        ),
        name="hidden_grads",
    )(place, row_counts, embed, own_squashed, side_parts, ids, prob)

    halved = keep + swap(give)

    near = [own_near, next_near, previous_near, opposite_near]
    far = [own_far, next_far, previous_far, opposite_far]
    half_spec = pl.BlockSpec((columns, HALF), lambda n, place, *_: (place[1], 0))
    embed_grad = pl.pallas_call(
        functools.partial(table_grad_kernel, rows, width),
        grid_spec=pltpu.PrefetchScalarGridSpec(
            num_scalar_prefetch=3,
            grid=(column_tiles,),
            in_specs=[
                pl.BlockSpec((COLUMN_TILE, BLOCK), lambda n, *_: (n, 0)),
                pl.BlockSpec((COLUMN_TILE, 2 * BLOCK), lambda n, *_: (n, 0)),
                pl.BlockSpec((COLUMN_TILE, BLOCK), lambda n, *_: (n, 0)),
                whole(side_parts.shape),
                whole(far_parts.shape),
                whole(ids.shape),
                whole(prob.shape),
                whole(packed_cot.shape),
                whole(packed_ids.shape),
            ]
            + [half_spec] * (2 * blocks),
            out_specs=pl.BlockSpec((columns, COLUMN_TILE), lambda n, *_: (0, n)),
            scratch_shapes=[
                pltpu.VMEM((blocks, columns, BLOCK), jnp.bfloat16),
                pltpu.VMEM((blocks - 1, COLUMN_TILE, BLOCK), jnp.bfloat16),
                pltpu.VMEM((blocks - 1, 1, BLOCK), jnp.float32),
            ],
        ),
        out_shape=shape_of((columns, rows), jnp.bfloat16),
        compiler_params=pltpu.CompilerParams(vmem_limit_bytes=36 << 20),
        cost_estimate=pl.CostEstimate(
            flops=2 * rows * columns * (tokens + BLOCK),
            bytes_accessed=rows * tokens * 4 + rows * columns * 2,
            transcendentals=rows * tokens,
        ),
        name="table_grads",
    )(
        place,
        column_counts,
        chunks,
        own_grads,
        side_squashed,
        far_squashed,
        side_parts,
        far_parts,
        ids,
        prob,
        packed_cot,
        packed_ids,
        *near,
        *far,
    )

    summed = jnp.sum(lax.all_to_all(halved, PLANE, 0, 0, tiled=True), axis=0)
    hidden_grad = summed[:thin].astype(jnp.bfloat16).T

    own_prob = jax.nn.softmax(teacher_logits, axis=1)
    first = vocab_index * share
    total = jnp.sum(side_parts[:, 0, :here], axis=0)
    own_total = lax.dynamic_slice_in_dim(total, first, share, 0)
    own_term = lax.dynamic_slice_in_dim(summed[thin], first, share, 0)
    divergence = (
        jnp.sum(own_prob * jnp.log(own_prob), axis=1) - own_term + jnp.log(own_total)
    )
    return (hidden_grad, embed_grad.T, divergence)


def solution(mesh):
    dp, vocab = (mesh.shape[name] for name in ("dp", "vocab"))
    side = math.isqrt(vocab // 2)
    fine = Mesh(mesh.devices.reshape(dp, side, side, 2), ("dp",) + RING)
    every = ("dp",) + RING
    return jax.shard_map(
        per_device,
        mesh=fine,
        in_specs=(
            P("dp", RING),
            P(RING, None),
            P("dp"),
            P("dp", RING),
            P(every, None),
            P(every, None),
        ),
        out_specs=(P("dp", RING), P(RING, "dp"), P(every)),
        check_vma=False,
    )
```

time: 632 us -> 229 us (0.36); the launches traced: 622 us -> 226 us
  waiting for transfers between devices: 353 us -> 27.9 us
  blocking collectives: 116 us -> 20.5 us
  Pallas kernels: 0 us -> 92.1 us
  matrix products: 72.2 us -> 0 us
  other arithmetic: 59.3 us -> 9.09 us
  starting transfers between devices: 0.16 us -> 45.1 us
  local copies, waits for them, and re-layouts: 7.19 us -> 30.3 us
  between operations: 14.2 us -> 1.03 us
    reduce_scatter x1 -> x0, waiting for transfers between devices: 317 us -> none  [per_device(): lax.psum_scatter(partial_rows, 'dp', scatter_dimension=1, tiled=True)]
    pallas_call x0 -> x7, Pallas kernels: none -> 92.1 us  [the longest x3 41 us: logits_call(): pl.pallas_call(functools.partial(logit_kernel, blocks), grid=(rows // ROW...]
    dot_general x4 -> x0, matrix products: 72.2 us -> none  [the longest x1 24.8 us: per_device(): lax.dot_general(onehot, cot_full, (((0,), (0,)), ((), ())), preferred_ele...]
    psum x1 -> x0, blocking collectives: 65.4 us -> none  [per_device(): total, term = lax.psum((part_total, part_term), 'vocab')]
    all_gather x2 -> x0, blocking collectives: 50.2 us -> none  [the longest x1 26.2 us: per_device(): lax.all_gather(teacher_logits, 'vocab', axis=0, tiled=True)]
    reduce_sum x6 -> x4, other arithmetic: 47.9 us -> 3.19 us  [the longest x1 1.4 us: per_device(): summed = jnp.sum(lax.all_to_all(halved, PLANE, 0, 0, tiled=True), axis=0)]
    unnamed x5 -> x0, waiting for transfers between devices: 36.5 us -> none
    all_to_all x0 -> x6, starting transfers between devices: none -> 34 us  [the longest x5 29.6 us: spread_to(): return lax.all_to_all(copies, axes, 0, 0, tiled=True)]
  transfers between devices with their start and end apart: 4 -> 17, of which waited for: 2 -> 6; matrix products, arithmetic and copies ran while one was open for 21% -> 6% of each run, Pallas kernels for 0% -> 41%
where the time goes in v2:
time: 229 us; the launch traced here: 226 us
  Pallas kernels  92.1 us (40%)
  starting transfers between devices  45.1 us (20%)
  local copies, waits for them, and re-layouts  30.3 us (13%)
  waiting for transfers between devices  27.9 us (12%)
  blocking collectives  20.5 us (9%)
  other arithmetic  9.09 us (4%)
    pallas_call x3, Pallas kernels, logits_call(): pl.pallas_call(functools.partial(logit_kernel, blocks), grid=(rows // ROW...  41 us
    all_to_all x5, starting transfers between devices, spread_to(): return lax.all_to_all(copies, axes, 0, 0, tiled=True)  29.6 us
    pallas_call x1, Pallas kernels, per_device(): pl.pallas_call(functools.partial(table_grad_kernel, rows, width), grid_sp...  27.6 us
    unnamed x59, local copies, waits for them, and re-layouts  23.4 us
    all_to_all x1, blocking collectives, spread_to(): return lax.all_to_all(copies, axes, 0, 0, tiled=True)  20.5 us
    pallas_call x1, Pallas kernels, per_device(): pl.pallas_call(hidden_grad_kernel, grid=(row_tiles,), in_specs=[smem(), s...  17.4 us
    ppermute x4, waiting for transfers between devices, shift(): lax.ppermute(value, 'dp', [(k, (k + by) % count) for k in range(count)])  14.8 us
    all_to_all x5, waiting for transfers between devices, spread_to(): return lax.all_to_all(copies, axes, 0, 0, tiled=True)  9.67 us
  transfers between devices with their start and end apart: 17, of which 6 were waited for; matrix products, arithmetic and copies ran while one was open for 6% of the time, Pallas kernels for 41%

profile of v2, /device:TPU:0, one launch (start us, length us, event | category | flops | bytes accessed | tf_op | source)
XLA Modules:
  0.0 226.1 jit_solution(9822503456649410194)
XLA Ops:
  2.8 20.5 %all_to_all.35 = bf16[16,144,128]{2,1,0:T(8,128)(2,1)S(1)} all-to-all(bf16[16,144,128]{2,1,0:T(8,128)(2,1)S(1)} %broadcast_in_dim.21), channel_id=1, replica_groups=mesh['dp'=4,'z'=4,'y'=4,'core'=2] {'z','y'}, dimensions={0} | all-to-all | bytes 1179648 | tf_op jit(solution)/shard_map/all_to_all | solution.py:310
  23.3 2.8 %collective-permute-start.2 = (bf16[2304,128]{1,0:T(8,128)(2,1)S(1)}, bf16[2304,128]{1,0:T(8,128)(2,1)S(1)}, u32[]{:S(2)}, u32[]{:S(2)}) collective-permute-start(bf16[2304,128]{1,0:T(8,128)(2,1)S(1)} %bitcast.18), channel_id=1, source_target_pairs={{0,96},{32,0},{64,32},{96,64},{1,97},{33,1},{65,33},{97,65},{2,98}... | collective-permute-start | bytes 1769480 | tf_op jit(solution)/shard_map/ppermute | solution.py:319
  26.2 11.4 %collective-permute-done.2.refs_0_.refs_1_ = bf16[2304,128]{1,0:T(8,128)(2,1)S(1)} collective-permute-done((bf16[2304,128]{1,0:T(8,128)(2,1)S(1)}, bf16[2304,128]{1,0:T(8,128)(2,1)S(1)}, u32[]{:S(2)}, u32[]{:S(2)}) %collective-permute-start.2) | collective-permute-done | bytes 589856 | tf_op jit(solution)/shard_map/ppermute | solution.py:319
  37.6 3.4 %collective-permute-done.3.refs_1_.refs_2_ = bf16[2304,128]{1,0:T(8,128)(2,1)S(1)} collective-permute-done((bf16[2304,128]{1,0:T(8,128)(2,1)S(1)}, bf16[2304,128]{1,0:T(8,128)(2,1)S(1)}, u32[]{:S(2)}, u32[]{:S(2)}) %collective-permute-start.3) | collective-permute-done | bytes 589856 | tf_op jit(solution)/shard_map/ppermute | solution.py:319
  41.7 3.9 %all-to-all-start = ((f32[4,16,128]{2,1,0:T(8,128)}), f32[4,16,128]{2,1,0:T(8,128)}, u32[]{:S(2)}, u32[]{:S(2)}) async-start(f32[4,16,128]{2,1,0:T(8,128)} %broadcast_in_dim.19), calls=%async_computation | async-start | bytes 65536 | tf_op jit(solution)/shard_map/all_to_all | solution.py:310
  45.6 5.4 %all-to-all-done = f32[4,16,128]{2,1,0:T(8,128)} async-done(((f32[4,16,128]{2,1,0:T(8,128)}), f32[4,16,128]{2,1,0:T(8,128)}, u32[]{:S(2)}, u32[]{:S(2)}) %all-to-all-start) | async-done | bytes 32800 | tf_op jit(solution)/shard_map/all_to_all | solution.py:310
  52.6 4.6 %all-to-all-start.1 = ((f32[32,4,8,128]{3,2,1,0:T(8,128)}), f32[32,4,8,128]{3,2,1,0:T(8,128)}, u32[]{:S(2)}, u32[]{:S(2)}) async-start(f32[32,4,8,128]{3,2,1,0:T(8,128)} %broadcast_in_dim.20), calls=%async_computation.1 | async-start | bytes 1048576 | tf_op jit(solution)/shard_map/all_to_all | solution.py:310
  57.3 12.4 %logits_1.2 = (f32[4000,256]{1,0:T(8,128)S(1)}, f32[1,256]{1,0:T(1,128)S(1)}) custom-call(s32[3]{0:T(128)S(1)} %pad_add_fusion.place, bf16[4000,2304]{1,0:T(8,128)(2,1)} %embed.7, bf16[2304,128]{1,0:T(8,128)(2,1)S(1)} %bitcast.21, bf16[2304,128]{1,0:T(8,128)(2,1)S(1)} %collective-permute-done.1.refs_1_.refs_4_), custom_call_target="tpu_custom_call" | custom-call | flops 4718592000 | bytes 22528000 | tf_op jit(solution)/shard_map/logits_1/pallas_call | solution.py:286
  69.7 2.0 copy-done.1
  71.7 16.1 %logits_2.1 = (f32[4000,512]{1,0:T(8,128)S(1)}, f32[1,512]{1,0:T(1,128)S(1)}) custom-call(s32[3]{0:T(128)S(1)} %pad_add_fusion.place, bf16[4000,2304]{1,0:T(8,128)(2,1)} %embed.7, bf16[2304,128]{1,0:T(8,128)(2,1)S(1)} %collective-permute-done.2.refs_0_.refs_1_, bf16[2304,128]{1,0:T(8,128)(2,1)S(1)} %collective-permute-done.3.refs_1_.refs_2_, ...), custom_call_target="tpu_custom_call" | custom-call | flops 9437184000 | bytes 26624000 | tf_op jit(solution)/shard_map/logits_2/pallas_call | solution.py:286
  87.9 3.2 %copy-done = f32[4000,512]{1,0:T(8,128)} copy-done((f32[4000,512]{1,0:T(8,128)}, f32[4000,512]{1,0:T(8,128)S(1)}, u32[]{:S(2)}) %copy-start) | copy-done | bytes 8192024
  91.8 7.3 %all-to-all-start.3 = ((f32[32,1,768]{2,1,0:T(1,128)}), f32[32,1,768]{2,1,0:T(1,128)S(1)}, u32[]{:S(2)}, u32[]{:S(2)}) async-start(f32[32,1,768]{2,1,0:T(1,128)} %broadcast_in_dim.23), calls=%async_computation.3 | async-start | bytes 196608 | tf_op jit(solution)/shard_map/all_to_all | solution.py:310
  99.1 1.4 collective-permute-start.7
  100.5 2.4 %teacher_prep.1 = (s32[4,64,256]{2,1,0:T(8,128)}, f32[4,64,256]{2,1,0:T(8,128)}, s32[10]{0:T(128)}, s32[24]{0:T(128)}) custom-call(s32[3]{0:T(128)} %copy-done.19, f32[32,4,8,128]{3,2,1,0:T(8,128)} %all-to-all-done.1.pack), custom_call_target="tpu_custom_call" | custom-call | tf_op jit(solution)/shard_map/teacher_prep/pallas_call | solution.py:387
  103.7 3.7 %collective-permute-start.8 = (bf16[1152,128]{1,0:T(8,128)(2,1)}, bf16[1152,128]{1,0:T(8,128)(2,1)}, u32[]{:S(2)}, u32[]{:S(2)}) collective-permute-start(bf16[1152,128]{1,0:T(8,128)(2,1)} %slice.42), channel_id=1, source_target_pairs={{0,32},{32,64},{64,96},{96,0},{1,33},{33,65},{65,97},{97,1},{2,34}... | collective-permute-start | bytes 884744 | tf_op jit(solution)/shard_map/ppermute | solution.py:319
  108.2 2.5 %collective-permute-start.9 = (bf16[1152,128]{1,0:T(8,128)(2,1)}, bf16[1152,128]{1,0:T(8,128)(2,1)S(1)}, u32[]{:S(2)}, u32[]{:S(2)}) collective-permute-start(bf16[1152,128]{1,0:T(8,128)(2,1)} %slice.43), channel_id=1, source_target_pairs={{0,96},{32,0},{64,32},{96,64},{1,97},{33,1},{65,33},{97,65},{2,98}... | collective-permute-start | bytes 884744 | tf_op jit(solution)/shard_map/ppermute | solution.py:319
  111.7 6.2 %all-to-all-start.5 = ((bf16[32,72,256]{2,1,0:T(8,128)(2,1)}), bf16[32,72,256]{2,1,0:T(8,128)(2,1)}, u32[]{:S(2)}, u32[]{:S(2)}) async-start(bf16[32,72,256]{2,1,0:T(8,128)(2,1)} %broadcast_in_dim.24), calls=%async_computation.5 | async-start | bytes 2359296 | tf_op jit(solution)/shard_map/all_to_all | solution.py:310
  118.0 2.2 copy-done.2
  120.2 17.4 %hidden_grads.1 = (bf16[4000,256]{1,0:T(8,128)(2,1)S(1)}, f32[16,80,256]{2,1,0:T(8,128)S(1)}, f32[16,80,256]{2,1,0:T(8,128)}) custom-call(s32[3]{0:T(128)S(1)} %copy-done.20, s32[10]{0:T(128)S(1)} %copy-done.23, bf16[4000,2304]{1,0:T(8,128)(2,1)} %embed.7, f32[4000,256]{1,0:T(8,128)S(1)} %copy-done.2, f32[32,1,768]{2,1,0:T(1,128)S(1)} %all-to-all-done.3.parts.side_parts, ...), custom_call_target="tpu_custom_call" | custom-call | flops 4718592000 | bytes 24576000 | tf_op jit(solution)/shard_map/hidden_grads/pallas_call | solution.py:412
  137.6 1.4 copy-done.5
  141.7 2.2 collective-permute-done.10.refs_1_.refs_7_
  143.9 12.4 %logits_1.3 = (f32[4000,256]{1,0:T(8,128)S(1)}, f32[1,256]{1,0:T(1,128)S(1)}) custom-call(s32[3]{0:T(128)S(1)} %copy-done.20, bf16[4000,2304]{1,0:T(8,128)(2,1)} %embed.7, bf16[2304,128]{1,0:T(8,128)(2,1)S(1)} %constant_dynamic-update-slice_fusion.refs_0_.refs_3_, bf16[2304,128]{1,0:T(8,128)(2,1)S(1)} %collective-permute-done.10.refs_1_.refs_7_), custom_call_target="tpu_custom_call" | custom-call | flops 4718592000 | bytes 22528000 | tf_op jit(solution)/shard_map/logits_1/pallas_call | solution.py:286
  156.4 2.0 copy-done.3
  159.0 7.6 %all-to-all-start.6 = ((f32[32,1,256]{2,1,0:T(1,128)}), f32[32,1,256]{2,1,0:T(1,128)}, u32[]{:S(2)}, u32[]{:S(2)}) async-start(f32[32,1,256]{2,1,0:T(1,128)} %broadcast_in_dim.26), calls=%async_computation.6 | async-start | bytes 65536 | tf_op jit(solution)/shard_map/all_to_all | solution.py:310
  166.6 2.9 %add.18 = f32[16,80,256]{2,1,0:T(8,128)} add(f32[16,80,256]{2,1,0:T(8,128)} %copy-done.7, f32[16,80,256]{2,1,0:T(8,128)} %collective-permute-done.6) | non-fusion elementwise | flops 327680 | bytes 3932160 | tf_op jit(solution)/shard_map/add | solution.py:448
  169.6 4.2 %all-to-all-done.6.far_parts = f32[32,1,256]{2,1,0:T(1,128)} async-done(((f32[32,1,256]{2,1,0:T(1,128)}), f32[32,1,256]{2,1,0:T(1,128)}, u32[]{:S(2)}, u32[]{:S(2)}) %all-to-all-start.6) | async-done | bytes 32800 | tf_op jit(solution)/shard_map/all_to_all | solution.py:310
  173.8 4.4 %all-to-all-start.4 = ((f32[16,80,256]{2,1,0:T(8,128)}), f32[16,80,256]{2,1,0:T(8,128)}, u32[]{:S(2)}, u32[]{:S(2)}) async-start(f32[16,80,256]{2,1,0:T(8,128)} %add.18), calls=%async_computation.4 | async-start | bytes 2621440 | tf_op jit(solution)/shard_map/all_to_all | solution.py:502
  180.7 3.7 %lookup_prep.1 = (bf16[4,576,256]{2,1,0:T(8,128)(2,1)}, s32[4,1,256]{2,1,0:T(1,128)}, s32[1]{0:T(128)}) custom-call(s32[3]{0:T(128)} %copy-done.19, s32[1,1024]{1,0:T(1,128)} %bitcast.26, bf16[4,576,256]{2,1,0:T(8,128)(2,1)} %bitcast.9.cot), custom_call_target="tpu_custom_call" | custom-call | tf_op jit(solution)/shard_map/lookup_prep/pallas_call | solution.py:400
  185.2 2.2 copy-done.4
  187.4 1.6 copy-done.6
  195.8 27.6 %table_grads.1 = bf16[576,4000]{1,0:T(8,128)(2,1)} custom-call(s32[3]{0:T(128)S(1)} %copy-done.21, s32[24]{0:T(128)S(1)} %copy-done.24, s32[1]{0:T(128)} %get-tuple-element.28.chunks, bf16[4000,256]{1,0:T(8,128)(2,1)S(1)} %copy-done.6, f32[4000,512]{1,0:T(8,128)} %copy-done, f32[4000,256]{1,0:T(8,128)S(1)} %copy-done.4, f32[32,1,768]{2,1,0:T(1,128)S(1)} %copy-done.10, ...), custom_call_target="tpu_custom_call" | custom-call | flops 5898240000 | bytes 20992000 | tf_op jit(solution)/shard_map/table_grads/pallas_call | solution.py:453
  223.4 1.4 reduce_sum.36
  (98 shorter events, 22.6 us)
Async XLA Ops:
  0.6 25.5 %copy-start.26 = (s32[8,64]{1,0:T(8,128)S(1)}, s32[8,64]{1,0:T(8,128)}, u32[]{:S(2)}) copy-start(s32[8,64]{1,0:T(8,128)} %param.10) | copy-start | bytes 6148
  0.6 25.6 %copy-start.28 = (s32[256]{0:T(256)S(1)}, s32[256]{0:T(256)}, u32[]{:S(2)}) copy-start(s32[256]{0:T(256)} %param.8) | copy-start | bytes 3076
  0.7 40.3 %copy-start.25 = (f32[8,64]{1,0:T(8,128)S(1)}, f32[8,64]{1,0:T(8,128)}, u32[]{:S(2)}) copy-start(f32[8,64]{1,0:T(8,128)} %param.11) | copy-start | bytes 6148
  1.4 1.3 collective-permute-start
  23.3 14.2 %collective-permute-start.2 = (bf16[2304,128]{1,0:T(8,128)(2,1)S(1)}, bf16[2304,128]{1,0:T(8,128)(2,1)S(1)}, u32[]{:S(2)}, u32[]{:S(2)}) collective-permute-start(bf16[2304,128]{1,0:T(8,128)(2,1)S(1)} %bitcast.18), channel_id=1, source_target_pairs={{0,96},{32,0},{64,32},{96,64},{1,97},{33,1},{65,33},{97,65},{2,98}... | collective-permute-start | bytes 1769480 | tf_op jit(solution)/shard_map/ppermute | solution.py:319
  26.1 14.9 %collective-permute-start.3 = (bf16[2304,128]{1,0:T(8,128)(2,1)S(1)}, bf16[2304,128]{1,0:T(8,128)(2,1)S(1)}, u32[]{:S(2)}, u32[]{:S(2)}) collective-permute-start(bf16[2304,128]{1,0:T(8,128)(2,1)S(1)} %bitcast.19), channel_id=1, source_target_pairs={{0,32},{32,64},{64,96},{96,0},{1,33},{33,65},{65,97},{97,1},{2,34}... | collective-permute-start | bytes 1769480 | tf_op jit(solution)/shard_map/ppermute | solution.py:319
  26.1 31.2 %collective-permute-start.1 = (bf16[2304,128]{1,0:T(8,128)(2,1)S(1)}, bf16[2304,128]{1,0:T(8,128)(2,1)S(1)}, u32[]{:S(2)}, u32[]{:S(2)}) collective-permute-start(bf16[2304,128]{1,0:T(8,128)(2,1)S(1)} %bitcast.20), channel_id=1, source_target_pairs={{0,1},{1,0},{2,3},{3,2},{4,5},{5,4},{6,7},{7,6},{8,9},{9,8},{10,11... | collective-permute-start | bytes 1769480 | tf_op jit(solution)/shard_map/ppermute | solution.py:314
  37.6 34.1 %collective-permute-start.4 = (bf16[2304,128]{1,0:T(8,128)(2,1)S(1)}, bf16[2304,128]{1,0:T(8,128)(2,1)S(1)}, u32[]{:S(2)}, u32[]{:S(2)}) collective-permute-start(bf16[2304,128]{1,0:T(8,128)(2,1)S(1)} %collective-permute-done.2.refs_0_.refs_1_), channel_id=1, source_target_pairs={{0,1},{1,0},{2,3},{3,2},{4,5},{5,4},{6,7},{7,6},{8,9},{9,8},{10,11... | collective-permute-start | bytes 1769480 | tf_op jit(solution)/shard_map/ppermute | solution.py:314
  41.0 30.7 %collective-permute-start.5 = (bf16[2304,128]{1,0:T(8,128)(2,1)S(1)}, bf16[2304,128]{1,0:T(8,128)(2,1)S(1)}, u32[]{:S(2)}, u32[]{:S(2)}) collective-permute-start(bf16[2304,128]{1,0:T(8,128)(2,1)S(1)} %collective-permute-done.3.refs_1_.refs_2_), channel_id=1, source_target_pairs={{0,1},{1,0},{2,3},{3,2},{4,5},{5,4},{6,7},{7,6},{8,9},{9,8},{10,11... | collective-permute-start | bytes 1769480 | tf_op jit(solution)/shard_map/ppermute | solution.py:314
  41.7 9.4 %all-to-all-start = ((f32[4,16,128]{2,1,0:T(8,128)}), f32[4,16,128]{2,1,0:T(8,128)}, u32[]{:S(2)}, u32[]{:S(2)}) async-start(f32[4,16,128]{2,1,0:T(8,128)} %broadcast_in_dim.19), calls=%async_computation | async-start | bytes 65536 | tf_op jit(solution)/shard_map/all_to_all | solution.py:310
  45.6 26.1 %copy-start.19 = (s32[3]{0:T(128)}, s32[3]{0:T(128)S(1)}, u32[]{:S(2)}) copy-start(s32[3]{0:T(128)S(1)} %pad_add_fusion.place) | copy-start | bytes 40
  52.6 38.5 %all-to-all-start.1 = ((f32[32,4,8,128]{3,2,1,0:T(8,128)}), f32[32,4,8,128]{3,2,1,0:T(8,128)}, u32[]{:S(2)}, u32[]{:S(2)}) async-start(f32[32,4,8,128]{3,2,1,0:T(8,128)} %broadcast_in_dim.20), calls=%async_computation.1 | async-start | bytes 1048576 | tf_op jit(solution)/shard_map/all_to_all | solution.py:310
  71.7 16.1 %copy-start.15 = (bf16[2304,128]{1,0:T(8,128)(2,1)}, bf16[2304,128]{1,0:T(8,128)(2,1)S(1)}, u32[]{:S(2)}) copy-start(bf16[2304,128]{1,0:T(8,128)(2,1)S(1)} %collective-permute-done.4.refs_2_.refs_5_) | copy-start | bytes 1769476
  71.7 16.1 %copy-start.17 = (bf16[2304,128]{1,0:T(8,128)(2,1)}, bf16[2304,128]{1,0:T(8,128)(2,1)S(1)}, u32[]{:S(2)}) copy-start(bf16[2304,128]{1,0:T(8,128)(2,1)S(1)} %collective-permute-done.5.refs_3_.refs_6_) | copy-start | bytes 1769476
  87.9 3.2 %copy-start = (f32[4000,512]{1,0:T(8,128)}, f32[4000,512]{1,0:T(8,128)S(1)}, u32[]{:S(2)}) copy-start(f32[4000,512]{1,0:T(8,128)S(1)} %get-tuple-element.30.side_squashed) | copy-start | bytes 24576004
  91.8 18.8 %all-to-all-start.3 = ((f32[32,1,768]{2,1,0:T(1,128)}), f32[32,1,768]{2,1,0:T(1,128)S(1)}, u32[]{:S(2)}, u32[]{:S(2)}) async-start(f32[32,1,768]{2,1,0:T(1,128)} %broadcast_in_dim.23), calls=%async_computation.3 | async-start | bytes 196608 | tf_op jit(solution)/shard_map/all_to_all | solution.py:310
  99.1 11.5 %collective-permute-start.7 = (bf16[72,256]{1,0:T(8,128)(2,1)}, bf16[72,256]{1,0:T(8,128)(2,1)S(1)}, u32[]{:S(2)}, u32[]{:S(2)}) collective-permute-start(bf16[72,256]{1,0:T(8,128)(2,1)} %bitcast.27), channel_id=1, source_target_pairs={{0,0},{1,1},{2,2},{3,3},{4,4},{5,5},{6,6},{7,7},{8,32},{9,33},{10,... | collective-permute-start | bytes 110600 | tf_op jit(solution)/shard_map/ppermute | solution.py:382
  103.7 36.6 %collective-permute-start.8 = (bf16[1152,128]{1,0:T(8,128)(2,1)}, bf16[1152,128]{1,0:T(8,128)(2,1)}, u32[]{:S(2)}, u32[]{:S(2)}) collective-permute-start(bf16[1152,128]{1,0:T(8,128)(2,1)} %slice.42), channel_id=1, source_target_pairs={{0,32},{32,64},{64,96},{96,0},{1,33},{33,65},{65,97},{97,1},{2,34}... | collective-permute-start | bytes 884744 | tf_op jit(solution)/shard_map/ppermute | solution.py:319
  108.2 33.1 %collective-permute-start.9 = (bf16[1152,128]{1,0:T(8,128)(2,1)}, bf16[1152,128]{1,0:T(8,128)(2,1)S(1)}, u32[]{:S(2)}, u32[]{:S(2)}) collective-permute-start(bf16[1152,128]{1,0:T(8,128)(2,1)} %slice.43), channel_id=1, source_target_pairs={{0,96},{32,0},{64,32},{96,64},{1,97},{33,1},{65,33},{97,65},{2,98}... | collective-permute-start | bytes 884744 | tf_op jit(solution)/shard_map/ppermute | solution.py:319
  110.6 7.3 %copy-start.9 = (f32[32,1,768]{2,1,0:T(1,128)}, f32[32,1,768]{2,1,0:T(1,128)S(1)}, u32[]{:S(2)}) copy-start(f32[32,1,768]{2,1,0:T(1,128)S(1)} %all-to-all-done.3.parts.side_parts) | copy-start | bytes 294916
  111.7 6.3 %copy-start.11 = (s32[4,64,256]{2,1,0:T(8,128)S(1)}, s32[4,64,256]{2,1,0:T(8,128)}, u32[]{:S(2)}) copy-start(s32[4,64,256]{2,1,0:T(8,128)} %get-tuple-element.23.ids) | copy-start | bytes 786436
  111.7 6.3 %copy-start.13 = (f32[4,64,256]{2,1,0:T(8,128)S(1)}, f32[4,64,256]{2,1,0:T(8,128)}, u32[]{:S(2)}) copy-start(f32[4,64,256]{2,1,0:T(8,128)} %get-tuple-element.24.prob) | copy-start | bytes 786436
  111.7 6.3 %copy-start.20 = (s32[3]{0:T(128)S(1)}, s32[3]{0:T(128)}, u32[]{:S(2)}) copy-start(s32[3]{0:T(128)} %copy-done.19) | copy-start | bytes 40
  111.7 6.3 %copy-start.23 = (s32[10]{0:T(128)S(1)}, s32[10]{0:T(128)}, u32[]{:S(2)}) copy-start(s32[10]{0:T(128)} %get-tuple-element.19.counts) | copy-start | bytes 124
  111.7 46.6 %all-to-all-start.5 = ((bf16[32,72,256]{2,1,0:T(8,128)(2,1)}), bf16[32,72,256]{2,1,0:T(8,128)(2,1)}, u32[]{:S(2)}, u32[]{:S(2)}) async-start(bf16[32,72,256]{2,1,0:T(8,128)(2,1)} %broadcast_in_dim.24), calls=%async_computation.5 | async-start | bytes 2359296 | tf_op jit(solution)/shard_map/all_to_all | solution.py:310
  140.1 26.6 %collective-permute-start.6 = (f32[16,80,256]{2,1,0:T(8,128)}, f32[16,80,256]{2,1,0:T(8,128)}, u32[]{:S(2)}, u32[]{:S(2)}) collective-permute-start(f32[16,80,256]{2,1,0:T(8,128)} %get-tuple-element.26), channel_id=1, source_target_pairs={{0,1},{1,0},{2,3},{3,2},{4,5},{5,4},{6,7},{7,6},{8,9},{9,8},{10,11... | collective-permute-start | bytes 3932168 | tf_op jit(solution)/shard_map/ppermute | solution.py:314
  141.3 2.6 %collective-permute-start.10 = (bf16[2304,128]{1,0:T(8,128)(2,1)S(1)}, bf16[2304,128]{1,0:T(8,128)(2,1)S(1)}, u32[]{:S(2)}, u32[]{:S(2)}) collective-permute-start(bf16[2304,128]{1,0:T(8,128)(2,1)S(1)} %constant_dynamic-update-slice_fusion.refs_0_.refs_3_), channel_id=1, source_target_pairs={{0,1},{1,0},{2,3},{3,2},{4,5},{5,4},{6,7},{7,6},{8,9},{9,8},{10,11... | collective-permute-start | bytes 1769480 | tf_op jit(solution)/shard_map/ppermute | solution.py:314
  159.0 14.8 %all-to-all-start.6 = ((f32[32,1,256]{2,1,0:T(1,128)}), f32[32,1,256]{2,1,0:T(1,128)}, u32[]{:S(2)}, u32[]{:S(2)}) async-start(f32[32,1,256]{2,1,0:T(1,128)} %broadcast_in_dim.26), calls=%async_computation.6 | async-start | bytes 65536 | tf_op jit(solution)/shard_map/all_to_all | solution.py:310
  169.6 15.6 %copy-start.21 = (s32[3]{0:T(128)S(1)}, s32[3]{0:T(128)}, u32[]{:S(2)}) copy-start(s32[3]{0:T(128)} %copy-done.19) | copy-start | bytes 40
  169.6 15.6 %copy-start.24 = (s32[24]{0:T(128)S(1)}, s32[24]{0:T(128)}, u32[]{:S(2)}) copy-start(s32[24]{0:T(128)} %get-tuple-element.27.counts) | copy-start | bytes 292
  173.8 49.6 %all-to-all-start.4 = ((f32[16,80,256]{2,1,0:T(8,128)}), f32[16,80,256]{2,1,0:T(8,128)}, u32[]{:S(2)}, u32[]{:S(2)}) async-start(f32[16,80,256]{2,1,0:T(8,128)} %add.18), calls=%async_computation.4 | async-start | bytes 2621440 | tf_op jit(solution)/shard_map/all_to_all | solution.py:502
  185.2 2.2 copy-start.4
  (14 other events, 19.1 us)
